TPU v7x, 128 devices: a whole 4x4x4 slice. The times are simulated.
128 devices in a mesh: replica: 4 (over y_hi, core), shard: 32 (over z, x, y_lo).
Axes of the slice: x: 4, y: 4 (y_hi: 2, y_lo: 2; y = y_hi * 2 + y_lo), z: 4, core: 2. Of those that a mesh axis runs over, the one named last changes fastest.
Arguments:
- tokens: bfloat16 [81920, 8192], P(('replica', 'shard')), may hold values from -6 to 6
- cotangent: bfloat16 [81920, 512], P(('replica', 'shard')), may hold values from -6 to 6
- inner_weight: float32 [4, 8192, 512], P('replica', 'shard'), may hold values from -6 to 6
- first_moment: float32 [4, 8192, 512], P('replica', 'shard'), may hold values from -6 to 6
- second_moment: float32 [4, 8192, 512], P('replica', 'shard'), may hold values from 0.05 to 5
- outer_params: float32 [8192, 128], P(('shard', 'replica')), may hold values from -6 to 6
- outer_momentum: float32 [8192, 128], P(('shard', 'replica')), may hold values from -4 to 4
- fragment: int32 [1], replicated, may hold values from 0 to 3
Outputs:
- keys: bfloat16 [81920, 512], P(('replica', 'shard'))
- input_grad: bfloat16 [81920, 8192], P(('replica', 'shard'))
- inner_next: float32 [4, 8192, 512], P('replica', 'shard')
- first_next: float32 [4, 8192, 512], P('replica', 'shard')
- second_next: float32 [4, 8192, 512], P('replica', 'shard')
- outer_next: float32 [8192, 128], P(('shard', 'replica'))
- momentum_next: float32 [8192, 128], P(('shard', 'replica'))
All inputs are finite; a program needn't handle non-finite values.
Results may differ from a plain program's by a relative error of at most 0.005.
Values may be sent and summed in bfloat16 or wider, within the bound.
A program may use at most 192 MiB of HBM per device.

v0:
```python
import jax
import jax.numpy as jnp
from jax import lax
from jax.sharding import PartitionSpec as P

beta_first = 0.9
beta_second = 0.95
adam_rate = 0.05
decay_rate = 0.1
adam_eps = 1e-08
correction_first = 0.9999734386011124
correction_second = 0.994079470779666
outer_rate = 0.7
outer_beta = 0.9
mixing_weight = 0.5


def adam_update(weight, grad, first_moment, second_moment):
    first_next = beta_first * first_moment + (1.0 - beta_first) * grad
    second_next = beta_second * second_moment + (1.0 - beta_second) * grad * grad
    step_size = (
        first_next / correction_first / (jnp.sqrt(second_next / correction_second) + adam_eps)
    )
    weight_next = weight - adam_rate * (step_size + decay_rate * weight)
    return (weight_next, first_next, second_next)


def nesterov(outer_params, outer_momentum, mean_inner):
    pseudo = outer_params - mean_inner
    momentum_next = outer_beta * outer_momentum + pseudo
    params_next = outer_params - outer_rate * (pseudo + outer_beta * momentum_next)
    return (params_next, momentum_next)


def local(
    tokens,
    cotangent,
    inner_weight,
    first_moment,
    second_moment,
    outer_params,
    outer_momentum,
    fragment,
):
    shard_count = lax.axis_size("shard")
    replica_count = lax.axis_size("replica")
    token_count = tokens.shape[0]
    model_width = tokens.shape[1]
    frag_width = outer_params.shape[1]
    scale = model_width ** (-0.5)
    grad_scale = (token_count * shard_count) ** (-0.5)
    weight = inner_weight[0]
    weight_low = weight.astype(jnp.bfloat16)
    piece = lax.all_gather(weight_low, "shard", axis=0, tiled=True)
    columns = tokens
    key_total = jnp.dot(columns, piece, preferred_element_type=jnp.float32)
    back_part = lax.dot_general(
        cotangent, piece, (((1,), (1,)), ((), ())), preferred_element_type=jnp.float32
    )
    input_total = back_part
    key_total, input_total = (key_total, input_total)
    keys = (key_total * scale).astype(jnp.bfloat16)
    input_grad = (input_total * scale).astype(jnp.bfloat16)
    columns = tokens
    grad_sum = lax.psum_scatter(
        lax.dot_general(
            columns, cotangent, (((0,), (0,)), ((), ())), preferred_element_type=jnp.float32
        ).astype(jnp.bfloat16),
        "shard",
        scatter_dimension=0,
        tiled=True,
    ).astype(jnp.float32)
    grad = grad_sum * grad_scale
    weight_next, first_next, second_next = adam_update(
        weight, grad, first_moment[0], second_moment[0]
    )
    first_col = fragment[0] * frag_width
    inner_block = lax.dynamic_slice_in_dim(weight_next, first_col, frag_width, 1)
    owned_total = lax.psum_scatter(inner_block, "replica", scatter_dimension=0, tiled=True)
    params_own, momentum_own = nesterov(outer_params, outer_momentum, owned_total / replica_count)
    outer_block = lax.all_gather(
        params_own.astype(jnp.bfloat16), "replica", axis=0, tiled=True
    ).astype(params_own.dtype)
    mixed = mixing_weight * inner_block + (1.0 - mixing_weight) * outer_block
    weight_final = lax.dynamic_update_slice_in_dim(weight_next, mixed, first_col, 1)
    return (
        keys,
        input_grad,
        weight_final[None],
        first_next[None],
        second_next[None],
        params_own,
        momentum_own,
    )


def solution(mesh):
    in_specs = (
        P(("replica", "shard"), None),
        P(("replica", "shard"), None),
        P("replica", "shard", None),
        P("replica", "shard", None),
        P("replica", "shard", None),
        P(("shard", "replica"), None),
        P(("shard", "replica"), None),
        P(),
    )
    out_specs = (
        P(("replica", "shard"), None),
        P(("replica", "shard"), None),
        P("replica", "shard", None),
        P("replica", "shard", None),
        P("replica", "shard", None),
        P(("shard", "replica"), None),
        P(("shard", "replica"), None),
    )
    return jax.shard_map(local, mesh=mesh, in_specs=in_specs, out_specs=out_specs, check_vma=False)
```

profile of v0, /device:TPU:1, one launch (start us, length us, event | category | flops | bytes accessed | tf_op | source)
XLA Modules:
  0.0 439.2 jit_solution(3055555692715658436)
XLA Ops:
  7.2 0.0 copy-start
  7.2 0.0 all-gather.2.cloned.1.call-start
  7.2 1.8 bitcast_convert_fusion
  9.1 0.0 all-gather.2.cloned.1.call-update
  9.1 0.0 reduce-scatter.3.cloned.1.call-start
  9.1 0.0 copy-done
  9.1 13.1 %convolution_convert_fusion = bf16[8192,512]{1,0:T(8,128)(2,1)} fusion(bf16[640,8192]{1,0:T(8,128)(2,1)} %param.8, bf16[640,512]{1,0:T(8,128)(2,1)S(1)} %copy-done), kind=kOutput, calls=%fused_computation.1 | convolution fusion | flops 5372903424 | bytes 19529728 | tf_op jit(solution)/shard_map/dot_general | solution.py:66
  22.2 0.0 reduce-scatter.3.cloned.1.call-update
  22.2 0.0 reduce-scatter.5.cloned.1.call-start
  22.9 0.0 copy-start.1
  22.9 0.0 copy-start.3
  22.9 0.0 copy-start.4
  23.0 178.9 %all-gather.2.cloned.1.call-done = bf16[8192,512]{1,0:T(8,128)(2,1)} async-done(((bf16[256,512]{1,0:T(8,128)(2,1)}), bf16[8192,512]{1,0:T(8,128)(2,1)}) %all-gather.2.cloned.1.call-update) | async-done | bytes 8388624 | tf_op jit(solution)/shard_map/all_gather | solution.py:54
  201.8 11.4 %fusion = bf16[640,512]{1,0:T(8,128)(2,1)} fusion(bf16[640,8192]{1,0:T(8,128)(2,1)} %param.8, bf16[8192,512]{1,0:T(8,128)(2,1)} %all-gather.2.cloned.1.call-done), kind=kOutput, calls=%fused_computation.3 | convolution fusion | flops 5369364480 | bytes 19529728 | tf_op jit(solution)/shard_map/dot_general | solution.py:56
  213.2 178.9 %reduce-scatter.3.cloned.1.call-done = bf16[256,512]{1,0:T(8,128)(2,1)} async-done(((bf16[8192,512]{1,0:T(8,128)(2,1)}), bf16[256,512]{1,0:T(8,128)(2,1)}) %reduce-scatter.3.cloned.1.call-update) | async-done | bytes 262160 | tf_op jit(solution)/shard_map/reduce_scatter | solution.py:65
  392.2 0.0 copy-done.1
  392.2 0.0 copy-done.3
  392.2 0.0 copy-done.4
  392.2 2.3 fusion.7
  394.5 0.7 constant_dynamic-slice_fusion
  395.2 0.0 reduce-scatter.5.cloned.1.call-update
  395.2 0.0 copy-start.5
  395.2 0.0 copy-start.6
  395.2 11.6 %multiply_convert_fusion = bf16[640,8192]{1,0:T(8,128)(2,1)} fusion(bf16[640,512]{1,0:T(8,128)(2,1)S(1)} %copy-done, bf16[8192,512]{1,0:T(8,128)(2,1)} %all-gather.2.cloned.1.call-done), kind=kOutput, calls=%fused_computation | convolution fusion | flops 5379194880 | bytes 19529728 | tf_op jit(solution)/shard_map/dot_general | solution.py:57
  406.9 15.8 %reduce-scatter.5.cloned.1.call-done = f32[64,128]{1,0:T(8,128)} async-done(((f32[256,128]{1,0:T(8,128)}), f32[64,128]{1,0:T(8,128)}) %reduce-scatter.5.cloned.1.call-update) | async-done | bytes 32784 | tf_op jit(solution)/shard_map/reduce_scatter | solution.py:79
  422.7 0.0 copy-done.5
  422.7 0.0 copy-done.6
  422.7 1.4 fusion.8
  424.1 7.7 %all_gather.7 = bf16[256,128]{1,0:T(8,128)(2,1)S(1)} all-gather(bf16[64,128]{1,0:T(8,128)(2,1)S(1)} %get-tuple-element.7), channel_id=1, replica_groups=mesh['replica'=4,'shard'=32] {'replica'}, dimensions={0}, use_global_device_ids=true | all-gather | bytes 81920 | tf_op jit(solution)/shard_map/all_gather | solution.py:81
  431.9 0.0 copy-start.2
  431.9 0.8 copy-done.2
  (2 shorter events, 0.1 us)
Async XLA Ops:
  7.2 2.0 copy-start
  7.2 194.6 %all-gather.2.cloned.1.call-start = ((), (), s32[]{:S(2)}) async-start(), calls=%async_computation.2 | async-start | bytes 8650752 | tf_op jit(solution)/shard_map/all_gather | solution.py:54
  9.1 383.1 %reduce-scatter.3.cloned.1.call-start = ((), (), s32[]{:S(2)}) async-start(), calls=%async_computation.3 | async-start | bytes 8650752 | tf_op jit(solution)/shard_map/reduce_scatter | solution.py:65
  22.2 400.5 %reduce-scatter.5.cloned.1.call-start = ((), (), s32[]{:S(2)}) async-start(), calls=%async_computation.4 | async-start | bytes 163840 | tf_op jit(solution)/shard_map/reduce_scatter | solution.py:79
  22.9 369.2 %copy-start.1 = (f32[1,256,512]{2,1,0:T(8,128)S(1)}, f32[1,256,512]{2,1,0:T(8,128)}, u32[]{:S(2)}) copy-start(f32[1,256,512]{2,1,0:T(8,128)} %param.10) | copy-start | bytes 1572868
  22.9 369.2 %copy-start.3 = (f32[1,256,512]{2,1,0:T(8,128)S(1)}, f32[1,256,512]{2,1,0:T(8,128)}, u32[]{:S(2)}) copy-start(f32[1,256,512]{2,1,0:T(8,128)} %param.12) | copy-start | bytes 1572868
  22.9 369.2 %copy-start.4 = (f32[1,256,512]{2,1,0:T(8,128)S(1)}, f32[1,256,512]{2,1,0:T(8,128)}, u32[]{:S(2)}) copy-start(f32[1,256,512]{2,1,0:T(8,128)} %param.11) | copy-start | bytes 1572868
  395.2 27.5 %copy-start.5 = (f32[64,128]{1,0:T(8,128)S(1)}, f32[64,128]{1,0:T(8,128)}, u32[]{:S(2)}) copy-start(f32[64,128]{1,0:T(8,128)} %param.13) | copy-start | bytes 98308
  395.2 27.5 %copy-start.6 = (f32[64,128]{1,0:T(8,128)S(1)}, f32[64,128]{1,0:T(8,128)}, u32[]{:S(2)}) copy-start(f32[64,128]{1,0:T(8,128)} %param.14) | copy-start | bytes 98308
  431.9 0.8 copy-start.2
Sparse Core Ops, SparseCore 0:
  10.2 191.5 all-gather.1
  204.8 187.3 reduce-scatter.2
  395.3 27.3 reduce-scatter.4
where the time goes:
time: 439 us
  waiting for transfers between devices  374 us (85%)
  matrix products  36.1 us (8%)
  between operations  14.5 us (3%)
  blocking collectives  7.74 us (2%)
  other arithmetic  5.59 us (1%)
    reduce_scatter x1, waiting for transfers between devices, local(): lax.psum_scatter(lax.dot_general(columns, cotangent, (((0,), (0,)), ((),...  179 us
    all_gather x1, waiting for transfers between devices, local(): piece = lax.all_gather(weight_low, 'shard', axis=0, tiled=True)  179 us
    reduce_scatter x1, waiting for transfers between devices, local(): lax.psum_scatter(inner_block, 'replica', scatter_dimension=0, tiled=True)  15.8 us
    dot_general x1, matrix products, local(): lax.dot_general(columns, cotangent, (((0,), (0,)), ((), ())), preferred_e...  13.1 us
    dot_general x1, matrix products, local(): lax.dot_general(cotangent, piece, (((1,), (1,)), ((), ())), preferred_ele...  11.6 us
    dot_general x1, matrix products, local(): key_total = jnp.dot(columns, piece, preferred_element_type=jnp.float32)  11.4 us
  transfers between devices with their start and end apart: 3, of which 3 were waited for; matrix products, arithmetic and copies ran while one was open for 8% of the time, Pallas kernels for 0%

commit v1 on v0

v1 whole, which is shorter than its diff:
```python
import functools

import jax
import jax.numpy as jnp
from jax import lax
from jax.experimental import pallas as pl
from jax.experimental.pallas import tpu as pltpu
from jax.sharding import PartitionSpec as P

MESH = pl.DeviceIdType.MESH
BF16 = jnp.bfloat16
F32 = jnp.float32

beta_first = 0.9
beta_second = 0.95
adam_rate = 0.05
decay_rate = 0.1
adam_eps = 1e-08
correction_first = 0.9999734386011124
correction_second = 0.994079470779666
outer_rate = 0.7
outer_beta = 0.9
mixing_weight = 0.5

D, KW, FRAGW, TOK, ROWS = 8192, 512, 128, 640, 256
NSHARD, NREP = 32, 4
SCALE = D ** (-0.5)
GRAD_SCALE = (TOK * NSHARD) ** (-0.5)
NSTREAM = 4
PART = ROWS // NSTREAM

LINKS = ("x+", "x-", "z+", "z-", "y")
BACK = {"x+": "x-", "x-": "x+", "z+": "z-", "z-": "z+", "y": "y"}
ROOT = (0, 0, 0)
NODES = [(x, y, z) for z in (2, 1, 3, 0) for x in (2, 1, 3, 0) for y in (1, 0)]
TREES = (("x", 1), ("z", 1), ("x", -1), ("z", -1))

SEND_US = 1.42
HOP_US = 2.0
GRAD_US = 0.45
KEYS_US = 0.45
ADD_US = 0.25
ISSUE_US = 0.05
DEPTH = 4


def tree_parent(tree, node):
    first, sign = tree
    x, y, z = node
    a, b = (x, z) if first == "x" else (z, x)
    second = "z" if first == "x" else "x"

    def back(v):
        if sign > 0:
            return {1: (0, "+"), 2: (1, "+"), 3: (0, "-")}[v]
        return {3: (0, "-"), 2: (3, "-"), 1: (0, "+")}[v]

    if b == 2 and y == 1 and a in (0, 2):
        a, y, b, link = a, 0, b, "y"
    elif b:
        b, way = back(b)
        link = second + way
    elif y:
        y, link = 0, "y"
    else:
        a, way = back(a)
        link = first + way
    return ((a, y, b) if first == "x" else (b, y, a)), link


def make_trees():
    parent, children = {}, {}
    for s, tree in enumerate(TREES):
        for node in NODES:
            children.setdefault((s, node), [])
        for node in NODES:
            if node != ROOT:
                up, link = tree_parent(tree, node)
                parent[s, node] = (up, link)
                children[s, up].append((node, link))
    return parent, children


PARENT, CHILDREN = make_trees()
EDGES = {key: i for i, key in enumerate(sorted(PARENT))}


def plan_links():
    def height(key):
        return 1 + max([height((key[0], c)) for c, _ in CHILDREN[key]], default=0)

    def weight(key):
        return 1 + sum(weight((key[0], c)) for c, _ in CHILDREN[key])

    def depth(key):
        return 0 if key[1] == ROOT else 1 + depth((key[0], PARENT[key][0]))

    grads_done = NSHARD * GRAD_US + 3.0
    waiting = {key: len(v) for key, v in CHILDREN.items()}
    latest = {key: 0.0 for key in CHILDREN}
    ready = {link: [] for link in LINKS}
    free = {link: 0.0 for link in LINKS}
    for s in range(NSTREAM):
        for node, link in CHILDREN[s, ROOT]:
            ready[link].append((0.0, "gather", s, node))
    for key in PARENT:
        if not waiting[key]:
            ready[BACK[PARENT[key][1]]].append((grads_done, "reduce") + key)
    sends, arrival, roots = [], {}, {}
    while any(ready.values()):
        at, link = min((max(free[k], min(r[0] for r in v)), k) for k, v in ready.items() if v)
        open_now = [r for r in ready[link] if r[0] <= at + 1e-9]

        def rank(r):
            key = r[2:]
            if r[1] == "reduce":
                return (1, depth(key), 0, -EDGES[key])
            return (0, height(key), weight(key), -EDGES[key])

        pick = max(open_now, key=rank)
        ready[link].remove(pick)
        _, kind, s, node = pick
        free[link] = at + SEND_US
        there = at + SEND_US + HOP_US
        sends.append((at, link, kind, s, node))
        arrival[kind, s, node] = there
        if kind == "gather":
            for child, way in CHILDREN[s, node]:
                ready[way].append((there, "gather", s, child))
        else:
            up = (s, PARENT[s, node][0])
            waiting[up] -= 1
            latest[up] = max(latest[up], there)
            if not waiting[up]:
                if up[1] == ROOT:
                    roots[s] = latest[up]
                else:
                    ready[BACK[PARENT[up][1]]].append((max(latest[up] + ADD_US, grads_done), "reduce") + up)
    return sends, arrival, max(roots.values())


def make_program():
    sends, arrival, roots_at = plan_links()
    full_at = {n: max(arrival["gather", s, n] for s in range(NSTREAM)) for n in NODES if n != ROOT}
    full_at[ROOT] = 0.0
    keys_left = sorted(NODES, key=lambda n: full_at[n])
    tail = [(roots_at, "update"), (roots_at + 6.0, "outer"), (roots_at + 12.0, "spread")]
    events = sorted([(t, 1, ("send",) + tuple(r)) for t, *r in sends] + [(t, 0, (n,)) for t, n in tail], key=lambda e: e[:2])
    program, now, grads = [], 0.0, 0
    for at, _, op in events:
        while True:
            if grads < NSHARD and (now + 0.5 * GRAD_US < at or op[0] != "send" or op[2] == "reduce"):
                program.append(("grad", grads))
                grads += 1
                now += GRAD_US
            elif grads == NSHARD and keys_left and full_at[keys_left[0]] < now and now + 0.5 * KEYS_US < at:
                program.append(("keys", keys_left.pop(0)))
                now += KEYS_US
            else:
                break
        now = max(now, at) + (ADD_US if op[0] == "send" and op[2] == "reduce" else ISSUE_US)
        program.append(op)
    program += [("keys", n) for n in keys_left]
    return program


def adam(weight, grad, first, second):
    first_next = beta_first * first + (1.0 - beta_first) * grad
    second_next = beta_second * second + (1.0 - beta_second) * grad * grad
    step = first_next / correction_first / (jnp.sqrt(second_next / correction_second) + adam_eps)
    return weight - adam_rate * (step + decay_rate * weight), first_next, second_next


def select_block(fragment, array):
    block = array[:, :FRAGW]
    for f in range(1, KW // FRAGW):
        block = jnp.where(fragment == f, array[:, f * FRAGW : (f + 1) * FRAGW], block)
    return block


def exchange_kernel(
    fragment_ref, tokens_hbm, cot_hbm, weight_hbm, first_hbm, second_hbm, outer_hbm, mom_hbm,
    full_hbm, keys_ref, grad_ref, block_ref, outer_ref, mom_ref,
    tokens, cot, weight, first, second, outer, mom, full, sums, landed, keys_acc, inner, peers, spread,
    in_sem, full_sem, send_sem, gather_sem, reduce_sem, peer_send, peer_recv, spread_send, spread_recv,
):
    shard, rep = lax.axis_index("shard"), lax.axis_index("replica")
    my, mx, mz = shard % 2, (shard // 2) % 4, shard // 8
    core, high = rep % 2, rep // 2

    def owner(node):
        x, y, z = node
        return (((mz + 4 - z) % 4) * 4 + (mx + 4 - x) % 4) * 2 + (my + y) % 2

    def shard_at(link):
        x, y, z = mx, my, mz
        if link == "y":
            y = 1 - y
        elif link[0] == "x":
            x = (x + (1 if link[1] == "+" else 3)) % 4
        else:
            z = (z + (1 if link[1] == "+" else 3)) % 4
        return (z * 4 + x) * 2 + y

    there = {link: {"shard": shard_at(link)} for link in LINKS}
    peer = [high * 2 + 1 - core, (1 - high) * 2 + core, (1 - high) * 2 + 1 - core]

    def local(src, dst, i):
        return pltpu.make_async_copy(src, dst, in_sem.at[i])

    loads = [
        local(weight_hbm.at[0], weight, 0),
        local(cot_hbm, cot, 1),
        local(tokens_hbm, tokens, 2),
        local(first_hbm.at[0], first, 3),
        local(second_hbm.at[0], second, 4),
        local(outer_hbm, outer, 5),
        local(mom_hbm, mom, 6),
    ]
    for copy in loads:
        copy.start()
    barrier = pltpu.get_barrier_semaphore()
    for link in LINKS:
        pl.semaphore_signal(barrier, inc=1, device_id=there[link], device_id_type=MESH)
    for p in peer:
        pl.semaphore_signal(barrier, inc=1, device_id={"replica": p}, device_id_type=MESH)
    loads[0].wait()
    full[shard] = weight[...].astype(BF16)
    pl.semaphore_wait(barrier, 8)

    def part(s):
        return pl.ds(s * PART, PART)

    issued = {link: [] for link in LINKS}
    waited = set()
    full_copies = []

    def send_copy(kind, s, node, slot):
        edge = EDGES[s, node]
        up, link = PARENT[s, node]
        if kind == "gather":
            where = full.at[owner(up), part(s)]
            return pltpu.make_async_remote_copy(
                src_ref=where, dst_ref=where, send_sem=send_sem.at[LINKS.index(link), slot],
                recv_sem=gather_sem.at[edge], device_id=there[link], device_id_type=MESH,
            )
        link = BACK[link]
        return pltpu.make_async_remote_copy(
            src_ref=sums.at[owner(node), part(s)], dst_ref=landed.at[edge],
            send_sem=send_sem.at[LINKS.index(link), slot],
            recv_sem=reduce_sem.at[edge], device_id=there[link], device_id_type=MESH,
        )

    def arrived(kind, s, node):
        if (kind, s, node) in waited or node == ROOT:
            return
        waited.add((kind, s, node))
        edge = EDGES[s, node]
        if kind == "gather":
            where = full.at[owner(node), part(s)]
            pltpu.make_async_copy(where, where, gather_sem.at[edge]).wait()
        else:
            where = landed.at[edge]
            pltpu.make_async_copy(where, where, reduce_sem.at[edge]).wait()

    def summed(s, node):
        total = sums[owner(node), part(s)].astype(F32)
        for child, _ in CHILDREN[s, node]:
            arrived("reduce", s, child)
            total = total + landed[EDGES[s, child]].astype(F32)
        return total

    def send(link, kind, s, node):
        if kind == "gather":
            arrived("gather", s, PARENT[s, node][0])
        elif CHILDREN[s, node]:
            sums[owner(node), part(s)] = summed(s, node).astype(BF16)
        line = issued[link]
        if len(line) >= DEPTH:
            line[-DEPTH].wait_send()
        copy = send_copy(kind, s, node, len(line) % DEPTH)
        copy.start()
        line.append(copy)

    def grad_tile(i, carry):
        z, x, y = (2 + i // 8) % 4, (2 + (i % 8) // 2) % 4, 1 - i % 2
        which = owner((x, y, z))
        cols = pl.ds(pl.multiple_of(which * ROWS, ROWS), ROWS)
        sums[which] = lax.dot_general(
            tokens[:, cols], cot[...], (((0,), (0,)), ((), ())), preferred_element_type=F32
        ).astype(BF16)
        return carry

    def keys_tile(node, begin):
        for s in range(NSTREAM):
            arrived("gather", s, node)
        which = owner(node)
        copy = pltpu.make_async_copy(full.at[which], full_hbm.at[which], full_sem.at[NODES.index(node)])
        copy.start()
        full_copies.append(copy)
        cols = pl.ds(pl.multiple_of(which * ROWS, ROWS), ROWS)
        term = jnp.dot(tokens[:, cols], full[which], preferred_element_type=F32)
        if begin:
            keys_acc[...] = term
        else:
            keys_acc[...] += term

    mine = pl.ds(pl.multiple_of(rep * (ROWS // NREP), ROWS // NREP), ROWS // NREP)

    def update():
        for s in range(NSTREAM):
            grad_ref[part(s), :] = summed(s, ROOT) * GRAD_SCALE
        for copy in loads[3:]:
            copy.wait()
        f = fragment_ref[0]
        inner[...] = adam(
            select_block(f, weight[...]), select_block(f, grad_ref[...]),
            select_block(f, first[...]), select_block(f, second[...]),
        )[0]
        for copy in to_peers():
            copy.start()

    def to_peers():
        return [
            pltpu.make_async_remote_copy(
                src_ref=inner.at[pl.ds(pl.multiple_of(p * (ROWS // NREP), ROWS // NREP), ROWS // NREP)],
                dst_ref=peers.at[k], send_sem=peer_send.at[k], recv_sem=peer_recv.at[k],
                device_id={"replica": p}, device_id_type=MESH,
            )
            for k, p in enumerate(peer)
        ]

    def to_all():
        return [
            pltpu.make_async_remote_copy(
                src_ref=spread.at[mine], dst_ref=spread.at[mine], send_sem=spread_send.at[k],
                recv_sem=spread_recv.at[k], device_id={"replica": p}, device_id_type=MESH,
            )
            for k, p in enumerate(peer)
        ]

    def outer_step():
        total = inner[mine]
        for k, copy in enumerate(to_peers()):
            copy.wait_recv()
            total = total + peers[k]
        pseudo = outer[...] - total / NREP
        mom_next = outer_beta * mom[...] + pseudo
        outer_next = outer[...] - outer_rate * (pseudo + outer_beta * mom_next)
        outer_ref[...] = outer_next
        mom_ref[...] = mom_next
        spread[mine] = outer_next
        for copy in to_all():
            copy.start()

    def spread_step():
        for k, p in enumerate(peer):
            rows = pl.ds(pl.multiple_of(p * (ROWS // NREP), ROWS // NREP), ROWS // NREP)
            pltpu.make_async_copy(spread.at[rows], spread.at[rows], spread_recv.at[k]).wait()
        block_ref[...] = spread[...]

    program = make_program()
    at, begin = 0, True
    while at < len(program):
        op = program[at]
        if op[0] == "grad":
            if op[1] == 0:
                loads[1].wait()
                loads[2].wait()
            n = 1
            while at + n < len(program) and program[at + n][0] == "grad":
                n += 1
            lax.fori_loop(op[1], op[1] + n, grad_tile, 0)
            at += n
            continue
        if op[0] == "send":
            send(*op[1:])
        elif op[0] == "keys":
            keys_tile(op[1], begin)
            begin = False
        else:
            {"update": update, "outer": outer_step, "spread": spread_step}[op[0]]()
        at += 1

    keys_ref[...] = (keys_acc[...] * SCALE).astype(BF16)
    for line in issued.values():
        for copy in line[-DEPTH:]:
            copy.wait_send()
    for copy in to_peers() + to_all():
        copy.wait_send()
    for copy in full_copies:
        copy.wait()


def finish_kernel(
    fragment_ref, cot_ref, full_ref, weight_ref, first_ref, second_ref, grad_ref, block_ref, keys_in, outer_in, mom_in,
    input_ref, keys_ref, inner_ref, first_out, second_out, outer_ref, mom_ref,
):
    total = lax.dot_general(cot_ref[...], full_ref[...], (((1,), (1,)), ((), ())), preferred_element_type=F32)
    input_ref[...] = (total * SCALE).astype(BF16)
    keys_ref[...] = keys_in[...]
    outer_ref[...] = outer_in[...]
    mom_ref[...] = mom_in[...]
    weight_next, first_next, second_next = adam(weight_ref[0], grad_ref[...], first_ref[0], second_ref[0])
    first_out[0] = first_next
    second_out[0] = second_next
    for f in range(KW // FRAGW):
        cols = slice(f * FRAGW, (f + 1) * FRAGW)
        old = weight_next[:, cols]
        mixed = mixing_weight * old + (1.0 - mixing_weight) * block_ref[...]
        inner_ref[0, :, cols] = jnp.where(fragment_ref[0] == f, mixed, old)


def exchange(fragment, tokens, cotangent, inner_weight, first_moment, second_moment, outer_params, outer_momentum):
    anyspace = pl.BlockSpec(memory_space=pl.ANY)
    vmem = pl.BlockSpec(memory_space=pltpu.VMEM)
    edges = len(EDGES)
    return pl.pallas_call(
        exchange_kernel,
        out_shape=(
            jax.ShapeDtypeStruct((NSHARD, ROWS, KW), BF16),
            jax.ShapeDtypeStruct((TOK, KW), BF16),
            jax.ShapeDtypeStruct((ROWS, KW), F32),
            jax.ShapeDtypeStruct((ROWS, FRAGW), F32),
            jax.ShapeDtypeStruct((ROWS // NREP, FRAGW), F32),
            jax.ShapeDtypeStruct((ROWS // NREP, FRAGW), F32),
        ),
        in_specs=[pl.BlockSpec(memory_space=pltpu.SMEM)] + [anyspace] * 7,
        out_specs=(anyspace, vmem, vmem, vmem, vmem, vmem),
        scratch_shapes=[
            pltpu.VMEM((TOK, D), BF16),
            pltpu.VMEM((TOK, KW), BF16),
            pltpu.VMEM((ROWS, KW), F32),
            pltpu.VMEM((ROWS, KW), F32),
            pltpu.VMEM((ROWS, KW), F32),
            pltpu.VMEM((ROWS // NREP, FRAGW), F32),
            pltpu.VMEM((ROWS // NREP, FRAGW), F32),
            pltpu.VMEM((NSHARD, ROWS, KW), BF16),
            pltpu.VMEM((NSHARD, ROWS, KW), BF16),
            pltpu.VMEM((edges, PART, KW), BF16),
            pltpu.VMEM((TOK, KW), F32),
            pltpu.VMEM((ROWS, FRAGW), F32),
            pltpu.VMEM((NREP - 1, ROWS // NREP, FRAGW), F32),
            pltpu.VMEM((ROWS, FRAGW), F32),
            pltpu.SemaphoreType.DMA((7,)),
            pltpu.SemaphoreType.DMA((NSHARD,)),
            pltpu.SemaphoreType.DMA((len(LINKS), DEPTH)),
            pltpu.SemaphoreType.DMA((edges,)),
            pltpu.SemaphoreType.DMA((edges,)),
            pltpu.SemaphoreType.DMA((NREP - 1,)),
            pltpu.SemaphoreType.DMA((NREP - 1,)),
            pltpu.SemaphoreType.DMA((NREP - 1,)),
            pltpu.SemaphoreType.DMA((NREP - 1,)),
        ],
        compiler_params=pltpu.CompilerParams(
            collective_id=0, has_side_effects=True, vmem_limit_bytes=56 * 2**20
        ),
        cost_estimate=pl.CostEstimate(
            flops=4 * TOK * D * KW, bytes_accessed=30 * 2**20, transcendentals=0
        ),
        name="exchange",
    )(fragment, tokens, cotangent, inner_weight, first_moment, second_moment, outer_params, outer_momentum)


def finish(fragment, cotangent, full, inner_weight, first_moment, second_moment, grad, block, keys, outer, mom):
    steps = 8
    rows, toks, own, cols = ROWS // steps, TOK // steps, ROWS // NREP // steps, D // steps

    def state():
        return pl.BlockSpec((1, rows, KW), lambda i: (0, i, 0))

    def flat(n, m):
        return pl.BlockSpec((n, m), lambda i: (i, 0))

    return pl.pallas_call(
        finish_kernel,
        grid=(steps,),
        out_shape=(
            jax.ShapeDtypeStruct((TOK, D), BF16),
            jax.ShapeDtypeStruct((TOK, KW), BF16),
            jax.ShapeDtypeStruct((1, ROWS, KW), F32),
            jax.ShapeDtypeStruct((1, ROWS, KW), F32),
            jax.ShapeDtypeStruct((1, ROWS, KW), F32),
            jax.ShapeDtypeStruct((ROWS // NREP, FRAGW), F32),
            jax.ShapeDtypeStruct((ROWS // NREP, FRAGW), F32),
        ),
        in_specs=[
            pl.BlockSpec(memory_space=pltpu.SMEM),
            pl.BlockSpec((TOK, KW), lambda i: (0, 0)),
            flat(cols, KW),
            state(), state(), state(),
            flat(rows, KW), flat(rows, FRAGW), flat(toks, KW), flat(own, FRAGW), flat(own, FRAGW),
        ],
        out_specs=(
            pl.BlockSpec((TOK, cols), lambda i: (0, i)),
            flat(toks, KW),
            state(), state(), state(),
            flat(own, FRAGW), flat(own, FRAGW),
        ),
        compiler_params=pltpu.CompilerParams(
            dimension_semantics=("arbitrary",), vmem_limit_bytes=40 * 2**20
        ),
        cost_estimate=pl.CostEstimate(flops=2 * TOK * D * KW, bytes_accessed=24 * 2**20, transcendentals=0),
        name="finish",
    )(fragment, cotangent, full, inner_weight, first_moment, second_moment, grad, block, keys, outer, mom)


def local_step(tokens, cotangent, inner_weight, first_moment, second_moment, outer_params, outer_momentum, fragment):
    full, keys, grad, block, outer, mom = exchange(
        fragment, tokens, cotangent, inner_weight, first_moment, second_moment, outer_params, outer_momentum
    )
    input_grad, keys, inner_next, first_next, second_next, outer_next, mom_next = finish(
        fragment, cotangent, full.reshape(D, KW), inner_weight, first_moment, second_moment, grad, block, keys, outer, mom
    )
    return keys, input_grad, inner_next, first_next, second_next, outer_next, mom_next


def solution(mesh):
    tokens = P(("replica", "shard"), None)
    state = P("replica", "shard", None)
    owned = P(("shard", "replica"), None)
    return jax.shard_map(
        local_step,
        mesh=mesh,
        in_specs=(tokens, tokens, state, state, state, owned, owned, P()),
        out_specs=(tokens, tokens, state, state, state, owned, owned),
        check_vma=False,
    )
```

time: 439 us -> 108 us (0.25)
  waiting for transfers between devices: 374 us -> 0 us
  Pallas kernels: 0 us -> 97.9 us
  matrix products: 36.1 us -> 0 us
  between operations: 14.5 us -> 1.37 us
  blocking collectives: 7.74 us -> 0 us
  local copies, waits for them, and re-layouts: 1.54 us -> 7.94 us
  other arithmetic: 5.59 us -> 0 us
    reduce_scatter x2 -> x0, waiting for transfers between devices: 195 us -> none  [the longest x1 179 us: local(): lax.psum_scatter(lax.dot_general(columns, cotangent, (((0,), (0,)), ((),...]
    all_gather x1 -> x0, waiting for transfers between devices: 179 us -> none  [local(): piece = lax.all_gather(weight_low, 'shard', axis=0, tiled=True)]
    pallas_call x0 -> x2, Pallas kernels: none -> 97.9 us  [the longest x1 89.1 us: exchange(): pl.pallas_call(exchange_kernel, out_shape=(jax.ShapeDtypeStruct((NSHARD,...]
    dot_general x3 -> x0, matrix products: 36.1 us -> none  [the longest x1 13.1 us: local(): lax.dot_general(columns, cotangent, (((0,), (0,)), ((), ())), preferred_e...]
    all_gather x1 -> x0, blocking collectives: 7.74 us -> none  [local(): lax.all_gather(params_own.astype(jnp.bfloat16), 'replica', axis=0, tiled=...]
    unnamed x15 -> x20, local copies, waits for them, and re-layouts: 0.86 us -> 7.94 us
  transfers between devices with their start and end apart: 3 -> 0, of which waited for: 3 -> 0; matrix products, arithmetic and copies ran while one was open for 8% -> 0% of each run, Pallas kernels for 0% -> 0%
where the time goes in v1:
time: 108 us; the launch traced here: 107 us
  Pallas kernels  97.9 us (91%)
  local copies, waits for them, and re-layouts  7.94 us (7%)
  between operations  1.37 us (1%)
    pallas_call x1, Pallas kernels, exchange(): pl.pallas_call(exchange_kernel, out_shape=(jax.ShapeDtypeStruct((NSHARD,...  89.1 us
    pallas_call x1, Pallas kernels, finish(): pl.pallas_call(finish_kernel, grid=(steps,), out_shape=(jax.ShapeDtypeStr...  8.8 us
    unnamed x20, local copies, waits for them, and re-layouts  7.94 us

profile of v1, /device:TPU:1, one launch (start us, length us, event | category | flops | bytes accessed | tf_op | source)
XLA Modules:
  0.0 107.2 jit_solution(13575201452180793164)
XLA Ops:
  1.3 0.0 copy-start
  1.3 0.0 copy-start.1
  1.3 0.0 copy-start.2
  1.3 0.0 copy-start.3
  1.3 89.1 %exchange.1 = (bf16[32,256,512]{2,1,0:T(8,128)(2,1)}, bf16[640,512]{1,0:T(8,128)(2,1)}, f32[256,512]{1,0:T(8,128)}, f32[256,128]{1,0:T(8,128)}, f32[64,128]{1,0:T(8,128)}, /*index=5*/f32[64,128]{1,0:T(8,128)}) custom-call(s32[1]{0:T(128)S(6)} %copy.15.fragment_ref, bf16[640,8192]{1,0:T(8,128)(2,1)} %tokens_hbm.1, bf16[640,512]{1,0:T(8,128)(2,1)} %cot_ref.1, ...), custom_call_target="tpu_custom_call" | custom-call | flops 10737418240 | bytes 31457280 | tf_op jit(solution)/shard_map/exchange/pallas_call | solution.py:418
  90.5 0.0 copy-done
  90.5 0.0 copy-done.1
  90.5 0.0 copy-done.2
  90.5 0.0 copy-done.3
  90.5 0.0 copy-start.4
  90.5 3.4 %copy-done.4 = bf16[32,256,512]{2,1,0:T(8,128)(2,1)S(1)} copy-done((bf16[32,256,512]{2,1,0:T(8,128)(2,1)S(1)}, bf16[32,256,512]{2,1,0:T(8,128)(2,1)}, u32[]{:S(2)}) %copy-start.4) | copy-done | bytes 8388632
  93.9 0.0 copy-start.5
  93.9 1.1 %copy-done.5 = bf16[640,512]{1,0:T(8,128)(2,1)S(1)} copy-done((bf16[640,512]{1,0:T(8,128)(2,1)S(1)}, bf16[640,512]{1,0:T(8,128)(2,1)}, u32[]{:S(2)}) %copy-start.5) | copy-done | bytes 655384
  95.0 0.0 copy-start.6
  95.0 1.0 copy-done.6
  96.0 0.0 copy-start.7
  96.0 0.9 copy-done.7
  96.9 0.0 copy-start.8
  96.9 0.8 copy-done.8
  97.7 0.0 copy-start.9
  97.7 0.8 copy-done.9
  98.4 8.8 %finish.1 = (bf16[640,8192]{1,0:T(8,128)(2,1)}, bf16[640,512]{1,0:T(8,128)(2,1)}, f32[1,256,512]{2,1,0:T(8,128)}, f32[1,256,512]{2,1,0:T(8,128)}, f32[1,256,512]...) custom-call(s32[1]{0:T(128)S(6)} %copy.15.fragment_ref, bf16[640,512]{1,0:T(8,128)(2,1)S(1)} %copy-done, ...), custom_call_target="tpu_custom_call" | custom-call | flops 5368709120 | bytes 25165824 | tf_op jit(solution)/shard_map/finish/pallas_call | solution.py:475
Async XLA Ops:
  1.3 89.2 %copy-start = (bf16[640,512]{1,0:T(8,128)(2,1)S(1)}, bf16[640,512]{1,0:T(8,128)(2,1)}, u32[]{:S(2)}) copy-start(bf16[640,512]{1,0:T(8,128)(2,1)} %cot_ref.1) | copy-start | bytes 1966084
  1.3 89.2 %copy-start.1 = (f32[1,256,512]{2,1,0:T(8,128)S(1)}, f32[1,256,512]{2,1,0:T(8,128)}, u32[]{:S(2)}) copy-start(f32[1,256,512]{2,1,0:T(8,128)} %weight_ref.1) | copy-start | bytes 1572868
  1.3 89.2 %copy-start.2 = (f32[1,256,512]{2,1,0:T(8,128)S(1)}, f32[1,256,512]{2,1,0:T(8,128)}, u32[]{:S(2)}) copy-start(f32[1,256,512]{2,1,0:T(8,128)} %first_ref.1) | copy-start | bytes 1572868
  1.3 89.2 %copy-start.3 = (f32[1,256,512]{2,1,0:T(8,128)S(1)}, f32[1,256,512]{2,1,0:T(8,128)}, u32[]{:S(2)}) copy-start(f32[1,256,512]{2,1,0:T(8,128)} %second_ref.1) | copy-start | bytes 1572868
  90.5 3.4 %copy-start.4 = (bf16[32,256,512]{2,1,0:T(8,128)(2,1)S(1)}, bf16[32,256,512]{2,1,0:T(8,128)(2,1)}, u32[]{:S(2)}) copy-start(bf16[32,256,512]{2,1,0:T(8,128)(2,1)} %get-tuple-element.20) | copy-start | bytes 25165828
  93.9 1.1 %copy-start.5 = (bf16[640,512]{1,0:T(8,128)(2,1)S(1)}, bf16[640,512]{1,0:T(8,128)(2,1)}, u32[]{:S(2)}) copy-start(bf16[640,512]{1,0:T(8,128)(2,1)} %get-tuple-element.23.keys_in) | copy-start | bytes 1966084
  95.0 1.0 copy-start.6
  96.0 0.9 copy-start.7
  96.9 0.8 copy-start.8
  97.7 0.8 copy-start.9

commit v2 on v1

--- a/solution.py
+++ b/solution.py
@@ -38,7 +38,7 @@
 SEND_US = 1.42
 HOP_US = 2.0
 GRAD_US = 0.45
-KEYS_US = 0.45
+TILE_US = 0.5
 ADD_US = 0.25
 ISSUE_US = 0.05
 DEPTH = 4
@@ -89,9 +89,6 @@
     def height(key):
         return 1 + max([height((key[0], c)) for c, _ in CHILDREN[key]], default=0)
 
-    def weight(key):
-        return 1 + sum(weight((key[0], c)) for c, _ in CHILDREN[key])
-
     def depth(key):
         return 0 if key[1] == ROOT else 1 + depth((key[0], PARENT[key][0]))
 
@@ -106,7 +103,7 @@
     for key in PARENT:
         if not waiting[key]:
             ready[BACK[PARENT[key][1]]].append((grads_done, "reduce") + key)
-    sends, arrival, roots = [], {}, {}
+    sends, arrival, roots, begun = [], {}, {}, {}
     while any(ready.values()):
         at, link = min((max(free[k], min(r[0] for r in v)), k) for k, v in ready.items() if v)
         open_now = [r for r in ready[link] if r[0] <= at + 1e-9]
@@ -115,7 +112,7 @@
             key = r[2:]
             if r[1] == "reduce":
                 return (1, depth(key), 0, -EDGES[key])
-            return (0, height(key), weight(key), -EDGES[key])
+            return (0, height(key) + begun.get(key[1], 0), 0, -EDGES[key])
 
         pick = max(open_now, key=rank)
         ready[link].remove(pick)
@@ -125,6 +122,7 @@
         sends.append((at, link, kind, s, node))
         arrival[kind, s, node] = there
         if kind == "gather":
+            begun[node] = begun.get(node, 0) + 1
             for child, way in CHILDREN[s, node]:
                 ready[way].append((there, "gather", s, child))
         else:
@@ -143,7 +141,7 @@
     sends, arrival, roots_at = plan_links()
     full_at = {n: max(arrival["gather", s, n] for s in range(NSTREAM)) for n in NODES if n != ROOT}
     full_at[ROOT] = 0.0
-    keys_left = sorted(NODES, key=lambda n: full_at[n])
+    tiles_left = sorted(NODES, key=lambda n: full_at[n])
     tail = [(roots_at, "update"), (roots_at + 6.0, "outer"), (roots_at + 12.0, "spread")]
     events = sorted([(t, 1, ("send",) + tuple(r)) for t, *r in sends] + [(t, 0, (n,)) for t, n in tail], key=lambda e: e[:2])
     program, now, grads = [], 0.0, 0
@@ -153,14 +151,14 @@
                 program.append(("grad", grads))
                 grads += 1
                 now += GRAD_US
-            elif grads == NSHARD and keys_left and full_at[keys_left[0]] < now and now + 0.5 * KEYS_US < at:
-                program.append(("keys", keys_left.pop(0)))
-                now += KEYS_US
+            elif grads == NSHARD and tiles_left and full_at[tiles_left[0]] < now and now + 0.5 * TILE_US < at:
+                program.append(("tile", tiles_left.pop(0)))
+                now += TILE_US
             else:
                 break
         now = max(now, at) + (ADD_US if op[0] == "send" and op[2] == "reduce" else ISSUE_US)
         program.append(op)
-    program += [("keys", n) for n in keys_left]
+    program += [("tile", n) for n in tiles_left]
     return program
 
 
@@ -180,9 +178,9 @@
 
 def exchange_kernel(
     fragment_ref, tokens_hbm, cot_hbm, weight_hbm, first_hbm, second_hbm, outer_hbm, mom_hbm,
-    full_hbm, keys_ref, grad_ref, block_ref, outer_ref, mom_ref,
-    tokens, cot, weight, first, second, outer, mom, full, sums, landed, keys_acc, inner, peers, spread,
-    in_sem, full_sem, send_sem, gather_sem, reduce_sem, peer_send, peer_recv, spread_send, spread_recv,
+    keys_ref, input_ref, inner_ref, first_ref, second_ref, outer_ref, mom_ref,
+    tokens, cot, weight, first, second, outer, mom, full, sums, landed, keys_acc, grad, inner, peers, spread,
+    in_sem, send_sem, gather_sem, reduce_sem, peer_send, peer_recv, spread_send, spread_recv,
 ):
     shard, rep = lax.axis_index("shard"), lax.axis_index("replica")
     my, mx, mz = shard % 2, (shard // 2) % 4, shard // 8
@@ -233,7 +231,6 @@
 
     issued = {link: [] for link in LINKS}
     waited = set()
-    full_copies = []
 
     def send_copy(kind, s, node, slot):
         edge = EDGES[s, node]
@@ -291,34 +288,34 @@
         ).astype(BF16)
         return carry
 
-    def keys_tile(node, begin):
+    def weight_tile(node, begin):
         for s in range(NSTREAM):
             arrived("gather", s, node)
         which = owner(node)
-        copy = pltpu.make_async_copy(full.at[which], full_hbm.at[which], full_sem.at[NODES.index(node)])
-        copy.start()
-        full_copies.append(copy)
         cols = pl.ds(pl.multiple_of(which * ROWS, ROWS), ROWS)
         term = jnp.dot(tokens[:, cols], full[which], preferred_element_type=F32)
         if begin:
             keys_acc[...] = term
         else:
             keys_acc[...] += term
+        back = lax.dot_general(cot[...], full[which], (((1,), (1,)), ((), ())), preferred_element_type=F32)
+        input_ref[:, cols] = (back * SCALE).astype(BF16)
 
     mine = pl.ds(pl.multiple_of(rep * (ROWS // NREP), ROWS // NREP), ROWS // NREP)
 
     def update():
         for s in range(NSTREAM):
-            grad_ref[part(s), :] = summed(s, ROOT) * GRAD_SCALE
+            grad[part(s), :] = summed(s, ROOT) * GRAD_SCALE
         for copy in loads[3:]:
             copy.wait()
         f = fragment_ref[0]
         inner[...] = adam(
-            select_block(f, weight[...]), select_block(f, grad_ref[...]),
+            select_block(f, weight[...]), select_block(f, grad[...]),
             select_block(f, first[...]), select_block(f, second[...]),
         )[0]
         for copy in to_peers():
             copy.start()
+        inner_ref[0], first_ref[0], second_ref[0] = adam(weight[...], grad[...], first[...], second[...])
 
     def to_peers():
         return [
@@ -357,7 +354,10 @@
         for k, p in enumerate(peer):
             rows = pl.ds(pl.multiple_of(p * (ROWS // NREP), ROWS // NREP), ROWS // NREP)
             pltpu.make_async_copy(spread.at[rows], spread.at[rows], spread_recv.at[k]).wait()
-        block_ref[...] = spread[...]
+        mixed = mixing_weight * inner[...] + (1.0 - mixing_weight) * spread[...]
+        for f in range(KW // FRAGW):
+            cols = slice(f * FRAGW, (f + 1) * FRAGW)
+            inner_ref[0, :, cols] = jnp.where(fragment_ref[0] == f, mixed, inner_ref[0, :, cols])
 
     program = make_program()
     at, begin = 0, True
@@ -375,8 +375,8 @@
             continue
         if op[0] == "send":
             send(*op[1:])
-        elif op[0] == "keys":
-            keys_tile(op[1], begin)
+        elif op[0] == "tile":
+            weight_tile(op[1], begin)
             begin = False
         else:
             {"update": update, "outer": outer_step, "spread": spread_step}[op[0]]()
@@ -388,27 +388,32 @@
             copy.wait_send()
     for copy in to_peers() + to_all():
         copy.wait_send()
-    for copy in full_copies:
+
+
+def finish_kernel(*refs):
+    half = (len(refs) - 1) // 2
+    sems = refs[-1]
+    copies = []
+    for src, dst in zip(refs[:half], refs[half:-1]):
+        cuts = 4 if src.size > 2**20 else 1
+        rows = src.shape[0] // cuts
+        for c in range(cuts):
+            where = pl.ds(c * rows, rows)
+            copies.append(pltpu.make_async_copy(src.at[where], dst.at[where], sems.at[len(copies)]))
+            copies[-1].start()
+    for copy in copies:
         copy.wait()
 
 
-def finish_kernel(
-    fragment_ref, cot_ref, full_ref, weight_ref, first_ref, second_ref, grad_ref, block_ref, keys_in, outer_in, mom_in,
-    input_ref, keys_ref, inner_ref, first_out, second_out, outer_ref, mom_ref,
-):
-    total = lax.dot_general(cot_ref[...], full_ref[...], (((1,), (1,)), ((), ())), preferred_element_type=F32)
-    input_ref[...] = (total * SCALE).astype(BF16)
-    keys_ref[...] = keys_in[...]
-    outer_ref[...] = outer_in[...]
-    mom_ref[...] = mom_in[...]
-    weight_next, first_next, second_next = adam(weight_ref[0], grad_ref[...], first_ref[0], second_ref[0])
-    first_out[0] = first_next
-    second_out[0] = second_next
-    for f in range(KW // FRAGW):
-        cols = slice(f * FRAGW, (f + 1) * FRAGW)
-        old = weight_next[:, cols]
-        mixed = mixing_weight * old + (1.0 - mixing_weight) * block_ref[...]
-        inner_ref[0, :, cols] = jnp.where(fragment_ref[0] == f, mixed, old)
+OUTS = (
+    ((TOK, KW), BF16),
+    ((TOK, D), BF16),
+    ((1, ROWS, KW), F32),
+    ((1, ROWS, KW), F32),
+    ((1, ROWS, KW), F32),
+    ((ROWS // NREP, FRAGW), F32),
+    ((ROWS // NREP, FRAGW), F32),
+)
 
 
 def exchange(fragment, tokens, cotangent, inner_weight, first_moment, second_moment, outer_params, outer_momentum):
@@ -417,16 +422,9 @@
     edges = len(EDGES)
     return pl.pallas_call(
         exchange_kernel,
-        out_shape=(
-            jax.ShapeDtypeStruct((NSHARD, ROWS, KW), BF16),
-            jax.ShapeDtypeStruct((TOK, KW), BF16),
-            jax.ShapeDtypeStruct((ROWS, KW), F32),
-            jax.ShapeDtypeStruct((ROWS, FRAGW), F32),
-            jax.ShapeDtypeStruct((ROWS // NREP, FRAGW), F32),
-            jax.ShapeDtypeStruct((ROWS // NREP, FRAGW), F32),
-        ),
+        out_shape=[pltpu.VMEM(shape, dtype) for shape, dtype in OUTS],
         in_specs=[pl.BlockSpec(memory_space=pltpu.SMEM)] + [anyspace] * 7,
-        out_specs=(anyspace, vmem, vmem, vmem, vmem, vmem),
+        out_specs=[vmem] * len(OUTS),
         scratch_shapes=[
             pltpu.VMEM((TOK, D), BF16),
             pltpu.VMEM((TOK, KW), BF16),
@@ -439,11 +437,11 @@
             pltpu.VMEM((NSHARD, ROWS, KW), BF16),
             pltpu.VMEM((edges, PART, KW), BF16),
             pltpu.VMEM((TOK, KW), F32),
+            pltpu.VMEM((ROWS, KW), F32),
             pltpu.VMEM((ROWS, FRAGW), F32),
             pltpu.VMEM((NREP - 1, ROWS // NREP, FRAGW), F32),
             pltpu.VMEM((ROWS, FRAGW), F32),
             pltpu.SemaphoreType.DMA((7,)),
-            pltpu.SemaphoreType.DMA((NSHARD,)),
             pltpu.SemaphoreType.DMA((len(LINKS), DEPTH)),
             pltpu.SemaphoreType.DMA((edges,)),
             pltpu.SemaphoreType.DMA((edges,)),
@@ -453,66 +451,33 @@
             pltpu.SemaphoreType.DMA((NREP - 1,)),
         ],
         compiler_params=pltpu.CompilerParams(
-            collective_id=0, has_side_effects=True, vmem_limit_bytes=56 * 2**20
+            collective_id=0, has_side_effects=True, vmem_limit_bytes=46 * 2**20
         ),
         cost_estimate=pl.CostEstimate(
-            flops=4 * TOK * D * KW, bytes_accessed=30 * 2**20, transcendentals=0
+            flops=6 * TOK * D * KW, bytes_accessed=30 * 2**20, transcendentals=0
         ),
         name="exchange",
     )(fragment, tokens, cotangent, inner_weight, first_moment, second_moment, outer_params, outer_momentum)
 
 
-def finish(fragment, cotangent, full, inner_weight, first_moment, second_moment, grad, block, keys, outer, mom):
-    steps = 8
-    rows, toks, own, cols = ROWS // steps, TOK // steps, ROWS // NREP // steps, D // steps
-
-    def state():
-        return pl.BlockSpec((1, rows, KW), lambda i: (0, i, 0))
-
-    def flat(n, m):
-        return pl.BlockSpec((n, m), lambda i: (i, 0))
-
+def finish(*arrays):
     return pl.pallas_call(
         finish_kernel,
-        grid=(steps,),
-        out_shape=(
-            jax.ShapeDtypeStruct((TOK, D), BF16),
-            jax.ShapeDtypeStruct((TOK, KW), BF16),
-            jax.ShapeDtypeStruct((1, ROWS, KW), F32),
-            jax.ShapeDtypeStruct((1, ROWS, KW), F32),
-            jax.ShapeDtypeStruct((1, ROWS, KW), F32),
-            jax.ShapeDtypeStruct((ROWS // NREP, FRAGW), F32),
-            jax.ShapeDtypeStruct((ROWS // NREP, FRAGW), F32),
-        ),
-        in_specs=[
-            pl.BlockSpec(memory_space=pltpu.SMEM),
-            pl.BlockSpec((TOK, KW), lambda i: (0, 0)),
-            flat(cols, KW),
-            state(), state(), state(),
-            flat(rows, KW), flat(rows, FRAGW), flat(toks, KW), flat(own, FRAGW), flat(own, FRAGW),
-        ],
-        out_specs=(
-            pl.BlockSpec((TOK, cols), lambda i: (0, i)),
-            flat(toks, KW),
-            state(), state(), state(),
-            flat(own, FRAGW), flat(own, FRAGW),
-        ),
-        compiler_params=pltpu.CompilerParams(
-            dimension_semantics=("arbitrary",), vmem_limit_bytes=40 * 2**20
-        ),
-        cost_estimate=pl.CostEstimate(flops=2 * TOK * D * KW, bytes_accessed=24 * 2**20, transcendentals=0),
+        out_shape=[pltpu.HBM(a.shape, a.dtype) for a in arrays],
+        in_specs=[pl.BlockSpec(memory_space=pltpu.VMEM)] * len(arrays),
+        out_specs=[pl.BlockSpec(memory_space=pltpu.HBM)] * len(arrays),
+        scratch_shapes=[pltpu.SemaphoreType.DMA((16,))],
+        compiler_params=pltpu.CompilerParams(vmem_limit_bytes=2 * 2**20),
+        cost_estimate=pl.CostEstimate(flops=0, bytes_accessed=13 * 2**20, transcendentals=0),
         name="finish",
-    )(fragment, cotangent, full, inner_weight, first_moment, second_moment, grad, block, keys, outer, mom)
+    )(*[pltpu.with_memory_space_constraint(a, pltpu.VMEM) for a in arrays])
 
 
 def local_step(tokens, cotangent, inner_weight, first_moment, second_moment, outer_params, outer_momentum, fragment):
-    full, keys, grad, block, outer, mom = exchange(
+    outs = exchange(
         fragment, tokens, cotangent, inner_weight, first_moment, second_moment, outer_params, outer_momentum
     )
-    input_grad, keys, inner_next, first_next, second_next, outer_next, mom_next = finish(
-        fragment, cotangent, full.reshape(D, KW), inner_weight, first_moment, second_moment, grad, block, keys, outer, mom
-    )
-    return keys, input_grad, inner_next, first_next, second_next, outer_next, mom_next
+    return tuple(finish(*outs))
 
 
 def solution(mesh):

time: 108 us -> 94.9 us (0.88)
  local copies, waits for them, and re-layouts: 7.94 us -> 0 us
  Pallas kernels: 97.9 us -> 93.4 us
    unnamed x20 -> x0, local copies, waits for them, and re-layouts: 7.94 us -> none
    pallas_call x2, Pallas kernels: 97.9 us -> 93.4 us  [the longest x1 88.6 us: exchange(): pl.pallas_call(exchange_kernel, out_shape=[pltpu.VMEM(shape, dtype) for s...]
where the time goes in v2:
time: 94.9 us; the launch traced here: 94.8 us
  Pallas kernels  93.4 us (98%)
  between operations  1.47 us (2%)
    pallas_call x1, Pallas kernels, exchange(): pl.pallas_call(exchange_kernel, out_shape=[pltpu.VMEM(shape, dtype) for s...  88.6 us
    pallas_call x1, Pallas kernels, finish(): pl.pallas_call(finish_kernel, out_shape=[pltpu.HBM(a.shape, a.dtype) for...  4.77 us

profile of v2, /device:TPU:1, one launch (start us, length us, event | category | flops | bytes accessed | tf_op | source)
XLA Modules:
  0.0 94.8 jit_solution(3963320967257178141)
XLA Ops:
  1.3 88.6 %exchange.1 = (bf16[640,512]{1,0:T(8,128)(2,1)S(1)}, bf16[640,8192]{1,0:T(8,128)(2,1)S(1)}, f32[1,256,512]{2,1,0:T(8,128)S(1)}, f32[1,256,512]{2,1,0:T(8,128)S(1...) custom-call(s32[1]{0:T(128)S(6)} %copy.15.fragment_ref, ...), custom_call_target="tpu_custom_call" | custom-call | flops 16106127360 | bytes 31457280 | tf_op jit(solution)/shard_map/exchange/pallas_call | solution.py:423
  89.9 4.8 %finish.1 = (bf16[640,512]{1,0:T(8,128)(2,1)}, bf16[640,8192]{1,0:T(8,128)(2,1)}, f32[1,256,512]{2,1,0:T(8,128)}, f32[1,256,512]{2,1,0:T(8,128)}, f32[1,256,512]...) custom-call(bf16[640,512]{1,0:T(8,128)(2,1)S(1)} %get-tuple-element.14.refs_0_, ...), custom_call_target="tpu_custom_call" | custom-call | bytes 13631488 | tf_op jit(solution)/shard_map/finish/pallas_call | solution.py:464

commit v3 on v2

--- a/solution.py
+++ b/solution.py
@@ -32,15 +32,25 @@
 LINKS = ("x+", "x-", "z+", "z-", "y")
 BACK = {"x+": "x-", "x-": "x+", "z+": "z-", "z-": "z+", "y": "y"}
 ROOT = (0, 0, 0)
-NODES = [(x, y, z) for z in (2, 1, 3, 0) for x in (2, 1, 3, 0) for y in (1, 0)]
+NODES = [(x, y, z) for z in (2, 3, 0, 1) for x in (2, 3, 0, 1) for y in (1, 0)]
 TREES = (("x", 1), ("z", 1), ("x", -1), ("z", -1))
 
 SEND_US = 1.42
-HOP_US = 2.0
-GRAD_US = 0.45
-TILE_US = 0.5
-ADD_US = 0.25
+HOP_US = 4.5
+LOAD_US = 4.0
+GRAD_US = 0.42
+GRAD_SLACK = 1.0
+TILE_US = 0.55
+TILE_SLACK = 0.6
+BACKLOG = 3
+ADD_US = 0.06
 ISSUE_US = 0.05
+REDUCE_FROM = 8.0
+GATHER_FROM = 99.0
+GATHER_TO = 99.0
+NEAR = 1.0
+MIX = 0.0
+SEED = 0
 DEPTH = 4
 
 
@@ -92,9 +102,9 @@
     def depth(key):
         return 0 if key[1] == ROOT else 1 + depth((key[0], PARENT[key][0]))
 
-    grads_done = NSHARD * GRAD_US + 3.0
+    grad_at = {node: LOAD_US + GRAD_US * GRAD_SLACK * (i + 1) for i, node in enumerate(NODES)}
     waiting = {key: len(v) for key, v in CHILDREN.items()}
-    latest = {key: 0.0 for key in CHILDREN}
+    latest = {key: grad_at[key[1]] for key in CHILDREN}
     ready = {link: [] for link in LINKS}
     free = {link: 0.0 for link in LINKS}
     for s in range(NSTREAM):
@@ -102,7 +112,7 @@
             ready[link].append((0.0, "gather", s, node))
     for key in PARENT:
         if not waiting[key]:
-            ready[BACK[PARENT[key][1]]].append((grads_done, "reduce") + key)
+            ready[BACK[PARENT[key][1]]].append((latest[key], "reduce") + key)
     sends, arrival, roots, begun = [], {}, {}, {}
     while any(ready.values()):
         at, link = min((max(free[k], min(r[0] for r in v)), k) for k, v in ready.items() if v)
@@ -110,9 +120,11 @@
 
         def rank(r):
             key = r[2:]
+            mixed = MIX * ((EDGES[key] * 37 + SEED) % 101) / 101
             if r[1] == "reduce":
-                return (1, depth(key), 0, -EDGES[key])
-            return (0, height(key) + begun.get(key[1], 0), 0, -EDGES[key])
+                first = REDUCE_FROM <= at and not GATHER_FROM <= at < GATHER_TO
+                return (1 if first else -1, depth(key) + mixed, -r[0], -EDGES[key])
+            return (0, height(key) + NEAR * begun.get(key[1], 0) + mixed, -r[0], -EDGES[key])
 
         pick = max(open_now, key=rank)
         ready[link].remove(pick)
@@ -133,7 +145,7 @@
                 if up[1] == ROOT:
                     roots[s] = latest[up]
                 else:
-                    ready[BACK[PARENT[up][1]]].append((max(latest[up] + ADD_US, grads_done), "reduce") + up)
+                    ready[BACK[PARENT[up][1]]].append((latest[up] + ADD_US, "reduce") + up)
     return sends, arrival, max(roots.values())
 
 
@@ -142,20 +154,29 @@
     full_at = {n: max(arrival["gather", s, n] for s in range(NSTREAM)) for n in NODES if n != ROOT}
     full_at[ROOT] = 0.0
     tiles_left = sorted(NODES, key=lambda n: full_at[n])
+    order = {node: i for i, node in enumerate(NODES)}
     tail = [(roots_at, "update"), (roots_at + 6.0, "outer"), (roots_at + 12.0, "spread")]
     events = sorted([(t, 1, ("send",) + tuple(r)) for t, *r in sends] + [(t, 0, (n,)) for t, n in tail], key=lambda e: e[:2])
     program, now, grads = [], 0.0, 0
     for at, _, op in events:
+        need = order[op[3 + 1]] + 1 if op[0] == "send" and op[2] == "reduce" else 0
         while True:
-            if grads < NSHARD and (now + 0.5 * GRAD_US < at or op[0] != "send" or op[2] == "reduce"):
-                program.append(("grad", grads))
-                grads += 1
-                now += GRAD_US
-            elif grads == NSHARD and tiles_left and full_at[tiles_left[0]] < now and now + 0.5 * TILE_US < at:
-                program.append(("tile", tiles_left.pop(0)))
-                now += TILE_US
+            if grads < max(need, NSHARD * (op[0] != "send")):
+                pass
+            elif grads < NSHARD and max(now, LOAD_US) + 0.5 * GRAD_US < at:
+                pass
+            elif grads == NSHARD and tiles_left and full_at[tiles_left[0]] < now:
+                backlog = sum(full_at[n] < now for n in tiles_left)
+                if now + TILE_SLACK * TILE_US < at or backlog > BACKLOG:
+                    program.append(("tile", tiles_left.pop(0)))
+                    now += TILE_US
+                    continue
+                break
             else:
                 break
+            program.append(("grad", grads))
+            now = max(now, LOAD_US) + GRAD_US
+            grads += 1
         now = max(now, at) + (ADD_US if op[0] == "send" and op[2] == "reduce" else ISSUE_US)
         program.append(op)
     program += [("tile", n) for n in tiles_left]
@@ -177,10 +198,10 @@
 
 
 def exchange_kernel(
-    fragment_ref, tokens_hbm, cot_hbm, weight_hbm, first_hbm, second_hbm, outer_hbm, mom_hbm,
+    fragment_hbm, tokens_hbm, cot_hbm, weight_hbm, first_hbm, second_hbm, outer_hbm, mom_hbm,
     keys_ref, input_ref, inner_ref, first_ref, second_ref, outer_ref, mom_ref,
-    tokens, cot, weight, first, second, outer, mom, full, sums, landed, keys_acc, grad, inner, peers, spread,
-    in_sem, send_sem, gather_sem, reduce_sem, peer_send, peer_recv, spread_send, spread_recv,
+    fragment_ref, tokens, cot, weight, first, second, outer, mom, full, sums, landed, keys_acc, grad, inner, peers, spread,
+    in_sem, send_sem, gather_sem, reduce_sem, peer_send, peer_recv, spread_send, spread_recv, ready,
 ):
     shard, rep = lax.axis_index("shard"), lax.axis_index("replica")
     my, mx, mz = shard % 2, (shard // 2) % 4, shard // 8
@@ -214,17 +235,27 @@
         local(second_hbm.at[0], second, 4),
         local(outer_hbm, outer, 5),
         local(mom_hbm, mom, 6),
+        local(fragment_hbm, fragment_ref, 7),
     ]
-    for copy in loads:
-        copy.start()
+    loads[0].start()
     barrier = pltpu.get_barrier_semaphore()
     for link in LINKS:
         pl.semaphore_signal(barrier, inc=1, device_id=there[link], device_id_type=MESH)
     for p in peer:
-        pl.semaphore_signal(barrier, inc=1, device_id={"replica": p}, device_id_type=MESH)
+        @pl.when(p > rep)
+        def _():
+            pl.semaphore_signal(barrier, inc=1, device_id={"replica": p}, device_id_type=MESH)
+
     loads[0].wait()
+    for copy in loads[1:]:
+        copy.start()
     full[shard] = weight[...].astype(BF16)
-    pl.semaphore_wait(barrier, 8)
+    pl.semaphore_wait(barrier, len(LINKS) + rep)
+    for p in peer:
+        @pl.when(p < rep)
+        def _():
+            pl.semaphore_signal(ready, inc=1, device_id={"replica": p}, device_id_type=MESH)
+
 
     def part(s):
         return pl.ds(s * PART, PART)
@@ -313,6 +344,11 @@
             select_block(f, weight[...]), select_block(f, grad[...]),
             select_block(f, first[...]), select_block(f, second[...]),
         )[0]
+
+        @pl.when(rep < NREP - 1)
+        def _():
+            pl.semaphore_wait(ready, NREP - 1 - rep)
+
         for copy in to_peers():
             copy.start()
         inner_ref[0], first_ref[0], second_ref[0] = adam(weight[...], grad[...], first[...], second[...])
@@ -423,9 +459,10 @@
     return pl.pallas_call(
         exchange_kernel,
         out_shape=[pltpu.VMEM(shape, dtype) for shape, dtype in OUTS],
-        in_specs=[pl.BlockSpec(memory_space=pltpu.SMEM)] + [anyspace] * 7,
+        in_specs=[anyspace] * 8,
         out_specs=[vmem] * len(OUTS),
         scratch_shapes=[
+            pltpu.SMEM((1,), jnp.int32),
             pltpu.VMEM((TOK, D), BF16),
             pltpu.VMEM((TOK, KW), BF16),
             pltpu.VMEM((ROWS, KW), F32),
@@ -441,7 +478,7 @@
             pltpu.VMEM((ROWS, FRAGW), F32),
             pltpu.VMEM((NREP - 1, ROWS // NREP, FRAGW), F32),
             pltpu.VMEM((ROWS, FRAGW), F32),
-            pltpu.SemaphoreType.DMA((7,)),
+            pltpu.SemaphoreType.DMA((8,)),
             pltpu.SemaphoreType.DMA((len(LINKS), DEPTH)),
             pltpu.SemaphoreType.DMA((edges,)),
             pltpu.SemaphoreType.DMA((edges,)),
@@ -449,6 +486,7 @@
             pltpu.SemaphoreType.DMA((NREP - 1,)),
             pltpu.SemaphoreType.DMA((NREP - 1,)),
             pltpu.SemaphoreType.DMA((NREP - 1,)),
+            pltpu.SemaphoreType.REGULAR,
         ],
         compiler_params=pltpu.CompilerParams(
             collective_id=0, has_side_effects=True, vmem_limit_bytes=46 * 2**20

time: 94.9 us -> 92.7 us (0.977)
  Pallas kernels: 93.4 us -> 91.1 us
    pallas_call x1, Pallas kernels: 88.6 us -> 86.3 us  [exchange(): pl.pallas_call(exchange_kernel, out_shape=[pltpu.VMEM(shape, dtype) for s...]
where the time goes in v3:
time: 92.7 us; the launch traced here: 92.5 us
  Pallas kernels  91.1 us (98%)
  between operations  1.45 us (2%)
    pallas_call x1, Pallas kernels, exchange(): pl.pallas_call(exchange_kernel, out_shape=[pltpu.VMEM(shape, dtype) for s...  86.3 us
    pallas_call x1, Pallas kernels, finish(): pl.pallas_call(finish_kernel, out_shape=[pltpu.HBM(a.shape, a.dtype) for...  4.77 us

profile of v3, /device:TPU:1, one launch (start us, length us, event | category | flops | bytes accessed | tf_op | source)
XLA Modules:
  0.0 92.5 jit_solution(16708567584460454154)
XLA Ops:
  1.3 86.3 %exchange.1 = (bf16[640,512]{1,0:T(8,128)(2,1)S(1)}, bf16[640,8192]{1,0:T(8,128)(2,1)S(1)}, f32[1,256,512]{2,1,0:T(8,128)S(1)}, f32[1,256,512]{2,1,0:T(8,128)S(1...) custom-call(s32[1]{0:T(128)S(6)} %copy.15.fragment_hbm, ...), custom_call_target="tpu_custom_call" | custom-call | flops 16106127360 | bytes 31457280 | tf_op jit(solution)/shard_map/exchange/pallas_call | solution.py:459
  87.6 4.8 %finish.1 = (bf16[640,512]{1,0:T(8,128)(2,1)}, bf16[640,8192]{1,0:T(8,128)(2,1)}, f32[1,256,512]{2,1,0:T(8,128)}, f32[1,256,512]{2,1,0:T(8,128)}, f32[1,256,512]...) custom-call(bf16[640,512]{1,0:T(8,128)(2,1)S(1)} %get-tuple-element.14.refs_0_, ...), custom_call_target="tpu_custom_call" | custom-call | bytes 13631488 | tf_op jit(solution)/shard_map/finish/pallas_call | solution.py:502

commit v4 on v3

--- a/solution.py
+++ b/solution.py
@@ -32,7 +32,8 @@
 LINKS = ("x+", "x-", "z+", "z-", "y")
 BACK = {"x+": "x-", "x-": "x+", "z+": "z-", "z-": "z+", "y": "y"}
 ROOT = (0, 0, 0)
-NODES = [(x, y, z) for z in (2, 3, 0, 1) for x in (2, 3, 0, 1) for y in (1, 0)]
+ORDER = (2, 1, 3, 0)
+NODES = [(x, y, z) for z in ORDER for x in ORDER for y in (1, 0)]
 TREES = (("x", 1), ("z", 1), ("x", -1), ("z", -1))
 
 SEND_US = 1.42
@@ -310,14 +311,12 @@
         copy.start()
         line.append(copy)
 
-    def grad_tile(i, carry):
-        z, x, y = (2 + i // 8) % 4, (2 + (i % 8) // 2) % 4, 1 - i % 2
-        which = owner((x, y, z))
+    def grad_tile(node):
+        which = owner(node)
         cols = pl.ds(pl.multiple_of(which * ROWS, ROWS), ROWS)
         sums[which] = lax.dot_general(
             tokens[:, cols], cot[...], (((0,), (0,)), ((), ())), preferred_element_type=F32
         ).astype(BF16)
-        return carry
 
     def weight_tile(node, begin):
         for s in range(NSTREAM):
@@ -403,13 +402,8 @@
             if op[1] == 0:
                 loads[1].wait()
                 loads[2].wait()
-            n = 1
-            while at + n < len(program) and program[at + n][0] == "grad":
-                n += 1
-            lax.fori_loop(op[1], op[1] + n, grad_tile, 0)
-            at += n
-            continue
-        if op[0] == "send":
+            grad_tile(NODES[op[1]])
+        elif op[0] == "send":
             send(*op[1:])
         elif op[0] == "tile":
             weight_tile(op[1], begin)

time: 92.7 us -> 90.1 us (0.972)
  Pallas kernels: 91.1 us -> 88.5 us
    pallas_call x1, Pallas kernels: 86.3 us -> 83.8 us  [exchange(): pl.pallas_call(exchange_kernel, out_shape=[pltpu.VMEM(shape, dtype) for s...]
where the time goes in v4:
time: 90.1 us; the launch traced here: 90 us
  Pallas kernels  88.5 us (98%)
  between operations  1.45 us (2%)
    pallas_call x1, Pallas kernels, exchange(): pl.pallas_call(exchange_kernel, out_shape=[pltpu.VMEM(shape, dtype) for s...  83.8 us
    pallas_call x1, Pallas kernels, finish(): pl.pallas_call(finish_kernel, out_shape=[pltpu.HBM(a.shape, a.dtype) for...  4.77 us

profile of v4, /device:TPU:1, one launch (start us, length us, event | category | flops | bytes accessed | tf_op | source)
XLA Modules:
  0.0 90.0 jit_solution(13196534189012448621)
XLA Ops:
  1.3 83.8 %exchange.1 = (bf16[640,512]{1,0:T(8,128)(2,1)S(1)}, bf16[640,8192]{1,0:T(8,128)(2,1)S(1)}, f32[1,256,512]{2,1,0:T(8,128)S(1)}, f32[1,256,512]{2,1,0:T(8,128)S(1...) custom-call(s32[1]{0:T(128)S(6)} %copy.15.fragment_hbm, ...), custom_call_target="tpu_custom_call" | custom-call | flops 16106127360 | bytes 31457280 | tf_op jit(solution)/shard_map/exchange/pallas_call | solution.py:453
  85.0 4.8 %finish.1 = (bf16[640,512]{1,0:T(8,128)(2,1)}, bf16[640,8192]{1,0:T(8,128)(2,1)}, f32[1,256,512]{2,1,0:T(8,128)}, f32[1,256,512]{2,1,0:T(8,128)}, f32[1,256,512]...) custom-call(bf16[640,512]{1,0:T(8,128)(2,1)S(1)} %get-tuple-element.14.refs_0_, ...), custom_call_target="tpu_custom_call" | custom-call | bytes 13631488 | tf_op jit(solution)/shard_map/finish/pallas_call | solution.py:496

commit v5 on v4

--- a/solution.py
+++ b/solution.py
@@ -156,7 +156,7 @@
     full_at[ROOT] = 0.0
     tiles_left = sorted(NODES, key=lambda n: full_at[n])
     order = {node: i for i, node in enumerate(NODES)}
-    tail = [(roots_at, "update"), (roots_at + 6.0, "outer"), (roots_at + 12.0, "spread")]
+    tail = [(roots_at, "update"), (roots_at + 9.0, "outer"), (roots_at + 18.0, "spread")]
     events = sorted([(t, 1, ("send",) + tuple(r)) for t, *r in sends] + [(t, 0, (n,)) for t, n in tail], key=lambda e: e[:2])
     program, now, grads = [], 0.0, 0
     for at, _, op in events:

time: 90.1 us -> 89.4 us (level)
  Pallas kernels: 88.5 us -> 87.1 us
    pallas_call x1, Pallas kernels: 83.8 us -> 82.3 us  [exchange(): pl.pallas_call(exchange_kernel, out_shape=[pltpu.VMEM(shape, dtype) for s...]
where the time goes in v5:
time: 89.4 us; the launch traced here: 88.5 us
  Pallas kernels  87.1 us (97%)
  between operations  1.45 us (2%)
    pallas_call x1, Pallas kernels, exchange(): pl.pallas_call(exchange_kernel, out_shape=[pltpu.VMEM(shape, dtype) for s...  82.3 us
    pallas_call x1, Pallas kernels, finish(): pl.pallas_call(finish_kernel, out_shape=[pltpu.HBM(a.shape, a.dtype) for...  4.77 us

profile of v5, /device:TPU:1, one launch (start us, length us, event | category | flops | bytes accessed | tf_op | source)
XLA Modules:
  0.0 88.5 jit_solution(14961657958201669403)
XLA Ops:
  1.3 82.3 %exchange.1 = (bf16[640,512]{1,0:T(8,128)(2,1)S(1)}, bf16[640,8192]{1,0:T(8,128)(2,1)S(1)}, f32[1,256,512]{2,1,0:T(8,128)S(1)}, f32[1,256,512]{2,1,0:T(8,128)S(1...) custom-call(s32[1]{0:T(128)S(6)} %copy.15.fragment_hbm, ...), custom_call_target="tpu_custom_call" | custom-call | flops 16106127360 | bytes 31457280 | tf_op jit(solution)/shard_map/exchange/pallas_call | solution.py:453
  83.6 4.8 %finish.1 = (bf16[640,512]{1,0:T(8,128)(2,1)}, bf16[640,8192]{1,0:T(8,128)(2,1)}, f32[1,256,512]{2,1,0:T(8,128)}, f32[1,256,512]{2,1,0:T(8,128)}, f32[1,256,512]...) custom-call(bf16[640,512]{1,0:T(8,128)(2,1)S(1)} %get-tuple-element.14.refs_0_, ...), custom_call_target="tpu_custom_call" | custom-call | bytes 13631488 | tf_op jit(solution)/shard_map/finish/pallas_call | solution.py:496
